TPU v7x, 32 devices: a whole 2x2x4 slice. The times are simulated.
32 devices in a mesh: dp: 4 (over y, core), expert: 8 (over z, x).
Axes of the slice: x: 2, y: 2, z: 4, core: 2. Of those that a mesh axis runs over, the one named last changes fastest.
Arguments:
- hidden_in: bfloat16 [2048, 7168], P(('dp', 'expert')), may hold values from -6 to 6
- norm_gain: float32 [7168], replicated, may hold values from 0.25 to 4
- route_logits: float32 [2048, 8], P(('dp', 'expert')), may hold values from -6 to 6
- expert_ids: int32 [2048, 8], P(('dp', 'expert')), may hold values from 0 to 255, as said below
- w_gate: bfloat16 [8, 7168, 2048], P('dp', None, 'expert'), may hold values from -0.0625 to 0.0625
- w_up: bfloat16 [8, 7168, 2048], P('dp', None, 'expert'), may hold values from -0.0625 to 0.0625
- w_down: bfloat16 [8, 2048, 7168], P('dp', 'expert'), may hold values from -0.125 to 0.125
- w_latent: bfloat16 [7168, 576], P(('dp', 'expert')), may hold values from -0.0625 to 0.0625
- kv_gain: float32 [512], replicated, may hold values from 0.25 to 4
- queries: bfloat16 [2048, 36864], P(('dp', 'expert')), may hold values from -240 to 240
- page_pool: bfloat16 [4096, 9216], P(('dp', 'expert')), may hold values from -6 to 6
- page_table: int32 [2048, 6], P(('dp', 'expert')), may hold values from 0 to 143
- kv_lengths: int32 [2048], P(('dp', 'expert')), may hold values from 1 to 96, 98304 in all
- migration: int32 [4, 8, 4, 4], P('dp', 'expert'), may hold values from 0 to 127
Outputs:
- hidden_out: bfloat16 [2048, 7168], P(('dp', 'expert'))
- attended: bfloat16 [2048, 32768], P(('dp', 'expert'))
Inputs may be any that keep to these rules, and one draw needn't show every extreme that they name: `expert_ids`: each row names 8 different experts, at most one of them below 8. The rows of one device name one window expert at most 4 times; in every draw one window expert is named exactly 4 times by the rows of every device.
All inputs are finite; a program needn't handle non-finite values. No bound on the sum of `kv_lengths` on one device may be relied on, other than what follows from the above.
Results may differ from a plain program's by a relative error of at most 0.038.
Values may be sent and summed in bfloat16 or wider, within the bound.
A program may use at most 192 MiB of HBM per device.

v0:
```python
import jax
import jax.numpy as jnp
from jax import lax
from jax.sharding import PartitionSpec as P

HEADS = 64
LATENT = 512
PAGE = 16
MAXP = 6
CAP = 4
MCAP = 4
KVW = 576


softmax_scale = 192.0 ** (-0.5)
routed_scale = 2.5
norm_eps = 1e-06


def rms_rows(values, gain):
    stat = jnp.mean(values * values, axis=-1, keepdims=True)
    return values * lax.rsqrt(stat + norm_eps) * gain


def rotate_keys(rope_part, position):
    half = rope_part.shape[1] // 2
    freq = 10000.0 ** (-jnp.arange(half, dtype=jnp.float32) / half)
    angle = position[:, None] * freq[None, :]
    first = rope_part[:, :half]
    second = rope_part[:, half:]
    cosine = jnp.cos(angle)
    sine = jnp.sin(angle)
    return jnp.concatenate([first * cosine - second * sine, second * cosine + first * sine], axis=1)


def body(
    hidden_in,
    norm_gain,
    route_logits,
    expert_ids,
    w_gate,
    w_up,
    w_down,
    w_latent,
    kv_gain,
    queries,
    page_pool,
    page_table,
    kv_lengths,
    migration,
):
    dp_count = lax.axis_size("dp")
    row_count = hidden_in.shape[0]
    local_experts = w_gate.shape[0]
    window = local_experts * dp_count
    width = hidden_in.shape[1]
    flat_list = migration.reshape(dp_count * MCAP)
    outgoing = jnp.take(page_pool, flat_list, axis=0).reshape(dp_count, MCAP, page_pool.shape[1])
    incoming = lax.all_to_all(outgoing, "dp", split_axis=0, concat_axis=0, tiled=True)
    x_wide = hidden_in.astype(jnp.float32)
    normed = rms_rows(x_wide, norm_gain).astype(jnp.bfloat16)
    in_window = expert_ids < window
    has = jnp.any(in_window, axis=1)
    chosen = jnp.sum(jnp.where(in_window, expert_ids, 0), axis=1)
    sigma = jax.nn.sigmoid(route_logits)
    weight = (
        routed_scale * jnp.sum(jnp.where(in_window, sigma, 0.0), axis=1) / jnp.sum(sigma, axis=1)
    )
    onehot = ((chosen[:, None] == jnp.arange(window)[None, :]) & has[:, None]).astype(jnp.int32)
    rank = jnp.cumsum(onehot, axis=0) - onehot
    slot = jnp.sum(rank * onehot, axis=1)
    group = chosen // local_experts
    within = chosen % local_experts
    send_index = within * (dp_count * CAP) + group * CAP + slot
    back_index = (group * CAP + slot) * local_experts + within
    slot_ids = jnp.arange(window * CAP)
    send_map = ((send_index[:, None] == slot_ids[None, :]) & has[:, None]).astype(jnp.bfloat16)
    back_map = ((back_index[:, None] == slot_ids[None, :]) & has[:, None]).astype(jnp.bfloat16)
    packed = jnp.einsum("rs,rd->sd", send_map, normed, preferred_element_type=jnp.float32).astype(
        jnp.bfloat16
    )
    packed = packed.reshape(local_experts, dp_count * CAP, width)
    arrived = lax.all_to_all(packed, "dp", split_axis=1, concat_axis=1, tiled=True)
    piece = lax.all_gather(arrived, "expert", axis=1, tiled=True)
    gate = jnp.einsum("end,edf->nef", piece, w_gate, preferred_element_type=jnp.float32)
    upper = jnp.einsum("end,edf->nef", piece, w_up, preferred_element_type=jnp.float32)
    active_all = (jax.nn.silu(gate) * upper).astype(jnp.bfloat16)
    summed = lax.psum_scatter(
        jnp.einsum("nef,efd->ned", active_all, w_down, preferred_element_type=jnp.float32).astype(
            jnp.bfloat16
        ),
        "expert",
        scatter_dimension=0,
        tiled=True,
    )
    returned = lax.all_to_all(summed, "dp", split_axis=0, concat_axis=0, tiled=True)
    picked = jnp.dot(
        back_map, returned.reshape(window * CAP, width), preferred_element_type=jnp.float32
    )
    hidden_out = (x_wide + weight[:, None] * picked).astype(jnp.bfloat16)
    projected = jnp.dot(
        hidden_out,
        lax.all_gather(w_latent, ("dp", "expert"), axis=0, tiled=True),
        preferred_element_type=jnp.float32,
    )
    latent = rms_rows(projected[:, :LATENT], kv_gain)
    rotary = rotate_keys(projected[:, LATENT:], kv_lengths.astype(jnp.float32))
    new_key = jnp.concatenate([latent, rotary], axis=1).astype(jnp.bfloat16)
    extended = jnp.concatenate(
        [page_pool, incoming.reshape(dp_count * MCAP, page_pool.shape[1])], axis=0
    )
    keys = jnp.take(extended, page_table.reshape(row_count * MAXP), axis=0).reshape(
        row_count, MAXP * PAGE, KVW
    )
    query = queries.reshape(row_count, HEADS, KVW)
    scores = (
        jnp.einsum("rhc,rtc->rht", query, keys, preferred_element_type=jnp.float32) * softmax_scale
    )
    own = (
        jnp.einsum("rhc,rc->rh", query, new_key, preferred_element_type=jnp.float32) * softmax_scale
    )
    valid = jnp.arange(MAXP * PAGE)[None, None, :] < kv_lengths[:, None, None]
    top = jnp.maximum(jnp.max(jnp.where(valid, scores, -1e30), axis=2), own)
    expo = jnp.where(valid, jnp.exp(scores - top[:, :, None]), 0.0)
    expo_own = jnp.exp(own - top)
    total = jnp.sum(expo, axis=2) + expo_own
    probs = (expo / total[:, :, None]).astype(jnp.bfloat16)
    probs_own = (expo_own / total).astype(jnp.bfloat16)
    result = jnp.einsum(
        "rht,rtc->rhc", probs, keys[:, :, :LATENT], preferred_element_type=jnp.float32
    )
    result = result + probs_own.astype(jnp.float32)[:, :, None] * new_key[:, None, :LATENT].astype(
        jnp.float32
    )
    attended = result.astype(jnp.bfloat16).reshape(row_count, HEADS * LATENT)
    return (hidden_out, attended)


def solution(mesh):
    return jax.shard_map(
        body,
        mesh=mesh,
        in_specs=(
            P(("dp", "expert"), None),
            P(),
            P(("dp", "expert"), None),
            P(("dp", "expert"), None),
            P("dp", None, "expert"),
            P("dp", None, "expert"),
            P("dp", "expert", None),
            P(("dp", "expert"), None),
            P(),
            P(("dp", "expert"), None),
            P(("dp", "expert"), None),
            P(("dp", "expert"), None),
            P(("dp", "expert")),
            P("dp", "expert", None, None),
        ),
        out_specs=(P(("dp", "expert"), None), P(("dp", "expert"), None)),
        check_vma=False,
    )
```

profile of v0, /device:TPU:0, one launch (start us, length us, event | category | flops | bytes accessed | tf_op | source)
XLA Modules:
  0.0 257.7 jit_solution(5085558807325633006)
XLA Ops:
  9.0 1.5 fusion.8
  10.9 1.6 convolution_convert_fusion.1
  13.0 12.2 %all_to_all.15 = bf16[2,16,7168]{2,0,1:T(2,128)(2,1)S(1)} all-to-all(bf16[2,16,7168]{2,0,1:T(2,128)(2,1)S(1)} %copy.37), channel_id=1, replica_groups=mesh['dp'=4,'expert'=8] {'dp'}, dimensions={1} | all-to-all | bytes 917504 | tf_op jit(solution)/shard_map/all_to_all | solution.py:83
  26.1 67.2 %all-gather.3.cloned.1.call-done = bf16[2,128,7168]{2,1,0:T(8,128)(2,1)} async-done(((bf16[2,16,7168]{2,1,0:T(8,128)(2,1)}), bf16[2,128,7168]{2,1,0:T(8,128)(2,1)}) %all-gather.3.cloned.1.call-update) | async-done | bytes 3670032 | tf_op jit(solution)/shard_map/all_gather | solution.py:84
  93.4 5.3 %convolution_bitcast_fusion.1 = f32[128,2,256]{2,0,1:T(8,128)S(1)} fusion(bf16[2,128,7168]{2,1,0:T(8,128)(2,1)} %all-gather.3.cloned.1.call-done, bf16[2,7168,256]{2,1,0:T(8,128)(2,1)} %param.18), kind=kOutput, calls=%fused_computation.24 | convolution fusion | flops 939524096 | bytes 11272192 | tf_op jit(solution)/shard_map/end,edf->nef/dot_general | solution.py:85
  98.7 10.3 %fusion = bf16[128,2,7168]{2,0,1:T(8,128)(2,1)} fusion(bf16[2,256,7168]{2,1,0:T(8,128)(2,1)} %param.20, bf16[2,128,7168]{2,1,0:T(8,128)(2,1)} %all-gather.3.cloned.1.call-done, bf16[2,7168,256]{2,1,0:T(8,128)(2,1)} %param.19, f32[128,2,256]{2,0,1:T(8,128)S(1)} %convolution_bitcast_fusion.1), kind=kOutput, calls=%fused_computation.3 | convolution fusion | flops 1881276416 | bytes 22282240 | tf_op jit(solution)/shard_map/nef,efd->ned/dot_general | solution.py:89
  109.7 0.9 copy-done
  111.5 0.9 broadcast_select_fusion.1
  112.4 3.5 %all-to-all-start.2 = ((bf16[4,4,9216]{2,1,0:T(4,128)(2,1)}), bf16[4,4,9216]{2,1,0:T(4,128)(2,1)S(1)}, u32[]{:S(2)}, u32[]{:S(2)}) async-start(bf16[4,4,9216]{2,1,0:T(4,128)(2,1)} %broadcast_select_fusion.1), calls=%async_computation.3 | async-start | bytes 589824 | tf_op jit(solution)/shard_map/all_to_all | solution.py:59
  116.4 9.9 %reshape.212 = bf16[64,64,576]{2,1,0:T(8,128)(2,1)} reshape(bf16[64,36864]{1,0:T(8,128)(2,1)} %param.23) | data formatting | bytes 9437184 | tf_op jit(solution)/shard_map/reshape | solution.py:115
  126.7 1.9 pad_maximum_fusion
  128.5 7.9 %gather_fusion.1 = bf16[384,9216]{1,0:T(8,128)(2,1)} fusion(bf16[144,9216]{1,0:T(8,128)(2,1)S(1)} %pad_maximum_fusion, s32[1024]{0:T(1024)S(1)} %pad_clamp_fusion), kind=kCustom, calls=%fused_computation.1 | custom fusion | bytes 14157312 | tf_op jit(solution)/shard_map/jit(_take)/gather | solution.py:112
  136.5 12.9 %gather.15 = bf16[64,96,576]{2,1,0:T(8,128)(2,1)} reshape(bf16[384,9216]{1,0:T(8,128)(2,1)} %gather_fusion.1) | data formatting | bytes 14155776 | tf_op jit(solution)/shard_map/jit(_take)/gather | solution.py:112
  149.4 7.2 %broadcast_select_fusion = bf16[64,96,576]{2,1,0:T(8,128)(2,1)} fusion(bf16[64,96,576]{2,1,0:T(8,128)(2,1)} %gather.15, pred[64,96]{1,0:T(8,128)(4,1)S(1)} %copy.40), kind=kLoop, calls=%fused_computation.9 | loop fusion | flops 3538944 | bytes 14161920 | tf_op jit(solution)/shard_map/jit(_take)/select_n | solution.py:112
  156.6 57.1 %reduce-scatter.2.cloned.1.call-done = bf16[16,2,7168]{2,0,1:T(8,128)(2,1)} async-done(((bf16[128,2,7168]{2,0,1:T(8,128)(2,1)}), bf16[16,2,7168]{2,0,1:T(8,128)(2,1)}) %reduce-scatter.2.cloned.1.call-update) | async-done | bytes 458768 | tf_op jit(solution)/shard_map/reduce_scatter | solution.py:88
  213.6 2.3 copy.39
  215.9 3.6 %all-to-all-start.1 = ((bf16[16,2,7168]{2,1,0:T(2,128)(2,1)}), bf16[16,2,7168]{2,1,0:T(2,128)(2,1)S(1)}, u32[]{:S(2)}, u32[]{:S(2)}) async-start(bf16[16,2,7168]{2,1,0:T(2,128)(2,1)} %copy.39), calls=%async_computation.2 | async-start | bytes 917504 | tf_op jit(solution)/shard_map/all_to_all | solution.py:96
  219.5 8.1 %select_reduce_fusion = (f32[64,64]{1,0:T(8,128)S(1)}, f32[64,96,64]{1,2,0:T(8,128)S(1)}) fusion(pred[64,96]{1,0:T(8,128)(4,1)S(1)} %iota_compare_fusion, bf16[64,96,576]{2,1,0:T(8,128)(2,1)} %broadcast_select_fusion, bf16[64,64,576]{2,1,0:T(8,128)(2,1)} %reshape.212), kind=kOutput, calls=%fused_computation.19 | convolution fusion | flops 454160384 | bytes 13391872 | tf_op jit(solution)/shard_map/rhc,rtc->rht/dot_general | solution.py:117
  227.9 1.6 fusion.2
  229.6 5.5 %fusion.61 = f32[64,576]{1,0:T(8,128)S(1)} fusion(bf16[64,7168]{1,0:T(8,128)(2,1)S(1)} %fusion.2, bf16[7168,576]{1,0:T(8,128)(2,1)} %all-gather.5.cloned.1.call-done), kind=kOutput, calls=%fused_computation.107 | convolution fusion | flops 528482304 | bytes 9322496 | tf_op jit(solution)/shard_map/dot_general | solution.py:101
  236.0 4.2 %fusion.27 = f32[64,1,64]{2,1,0:T(1,128)S(1)} fusion(bf16[64,64,576]{2,1,0:T(8,128)(2,1)} %reshape.212, bf16[64,576,1]{1,0,2:T(8,128)(2,1)S(1)} %maximum_bitcast_fusion), kind=kOutput, calls=%fused_computation.40 | convolution fusion | flops 4718592 | bytes 4808704 | tf_op jit(solution)/shard_map/rhc,rc->rh/dot_general | solution.py:120
  240.2 1.3 bitcast_reduce_fusion
  241.6 4.0 %add_convert_fusion = bf16[64,64,512]{2,1,0:T(8,128)(2,1)S(1)} fusion(f32[64,512]{1,0:T(8,128)S(1)} %get-tuple-element.4, f32[64,64]{1,0:T(8,128)S(1)} %get-tuple-element.12, bf16[64,96,576]{2,1,0:T(8,128)(2,1)} %broadcast_select_fusion, f32[64,96,64]{1,2,0:T(8,128)S(1)} %get-tuple-element.16, f32[64,64]{1,0:T(8,128)S(1)} %get-tuple-element.11, ...), kind=kOutput, calls=%fused_computation.4 | convolution fusion | flops 410910720 | bytes 12244992 | tf_op jit(solution)/shard_map/rht,rtc->rhc/dot_general | solution.py:129
  245.6 4.6 %copy.50 = bf16[8,8,64,512]{3,1,2,0:T(8,128)(2,1)} copy(bf16[8,8,64,512]{3,2,1,0:T(8,128)(2,1)S(1)} %bitcast.44) | data formatting | bytes 8388608
  (66 shorter events, 6.3 us)
Async XLA Ops:
  8.0 85.4 %all-gather.3.cloned.1.call-start = ((), (), s32[]{:S(2)}) async-start(), calls=%async_computation.4 | async-start | bytes 4128768 | tf_op jit(solution)/shard_map/all_gather | solution.py:84
  26.1 187.5 %reduce-scatter.2.cloned.1.call-start = ((), (), s32[]{:S(2)}) async-start(), calls=%async_computation.5 | async-start | bytes 4128768 | tf_op jit(solution)/shard_map/reduce_scatter | solution.py:88
  108.9 0.7 copy-start.3
  108.9 1.7 copy-start
  109.0 6.9 %copy-start.4 = (f32[64,8]{0,1:T(8,128)S(1)}, f32[64,8]{0,1:T(8,128)}, u32[]{:S(2)}) copy-start(f32[64,8]{0,1:T(8,128)} %param.16) | copy-start | bytes 6148
  109.0 7.0 %copy-start.2 = (s32[64,6]{0,1:T(8,128)S(1)}, s32[64,6]{0,1:T(8,128)}, u32[]{:S(2)}) copy-start(s32[64,6]{0,1:T(8,128)} %param.25) | copy-start | bytes 4612
  109.0 120.6 %all-gather.5.cloned.1.call-start = ((), (), s32[]{:S(2)}) async-start(), calls=%async_computation.6 | async-start | bytes 9461760 | tf_op jit(solution)/shard_map/all_gather | solution.py:103
  112.4 14.2 %all-to-all-start.2 = ((bf16[4,4,9216]{2,1,0:T(4,128)(2,1)}), bf16[4,4,9216]{2,1,0:T(4,128)(2,1)S(1)}, u32[]{:S(2)}, u32[]{:S(2)}) async-start(bf16[4,4,9216]{2,1,0:T(4,128)(2,1)} %broadcast_select_fusion.1), calls=%async_computation.3 | async-start | bytes 589824 | tf_op jit(solution)/shard_map/all_to_all | solution.py:59
  116.3 10.0 %copy-start.6 = (s32[64]{0:T(128)S(1)}, s32[64]{0:T(128)}, u32[]{:S(2)}) copy-start(s32[64]{0:T(128)} %param.26) | copy-start | bytes 772
  215.9 11.8 %all-to-all-start.1 = ((bf16[16,2,7168]{2,1,0:T(2,128)(2,1)}), bf16[16,2,7168]{2,1,0:T(2,128)(2,1)S(1)}, u32[]{:S(2)}, u32[]{:S(2)}) async-start(bf16[16,2,7168]{2,1,0:T(2,128)(2,1)} %copy.39), calls=%async_computation.2 | async-start | bytes 917504 | tf_op jit(solution)/shard_map/all_to_all | solution.py:96
  229.5 5.6 %copy-start.1 = (bf16[64,7168]{1,0:T(8,128)(2,1)}, bf16[64,7168]{1,0:T(8,128)(2,1)S(1)}, u32[]{:S(2)}) copy-start(bf16[64,7168]{1,0:T(8,128)(2,1)S(1)} %fusion.2) | copy-start | bytes 2752516
  229.5 6.3 %copy-start.5 = (f32[512]{0:T(512)S(1)}, f32[512]{0:T(512)}, u32[]{:S(2)}) copy-start(f32[512]{0:T(512)} %param.22) | copy-start | bytes 6148
Sparse Core Ops, SparseCore 0:
  26.2 67.1 all-gather.2
  109.1 104.4 reduce-scatter.1
Sparse Core Ops, SparseCore 1:
  112.3 98.0 all-gather.4
where the time goes:
time: 259 us; the launch traced here: 258 us
  waiting for transfers between devices  125 us (48%)
  local copies, waits for them, and re-layouts  42.7 us (16%)
  matrix products  40.7 us (16%)
  between operations  15.8 us (6%)
  other arithmetic  14.1 us (5%)
  blocking collectives  12.2 us (5%)
  starting transfers between devices  7.23 us (3%)
    all_gather x1, waiting for transfers between devices, body(): piece = lax.all_gather(arrived, 'expert', axis=1, tiled=True)  67.2 us
    reduce_scatter x1, waiting for transfers between devices, body(): lax.psum_scatter(jnp.einsum('nef,efd->ned', active_all, w_down, preferred...  57.1 us
    gather x2, local copies, waits for them, and re-layouts, body(): jnp.take(extended, page_table.reshape(row_count * MAXP), axis=0)  20.9 us
    all_to_all x1, blocking collectives, body(): lax.all_to_all(packed, 'dp', split_axis=1, concat_axis=1, tiled=True)  12.2 us
    dot_general x1, matrix products, body(): jnp.einsum('nef,efd->ned', active_all, w_down, preferred_element_type=jnp...  10.3 us
    reshape x1, local copies, waits for them, and re-layouts, body(): query = queries.reshape(row_count, HEADS, KVW)  9.94 us
    dot_general x1, matrix products, body(): jnp.einsum('rhc,rtc->rht', query, keys, preferred_element_type=jnp.float32)  8.15 us
    select_n x2, other arithmetic, body(): jnp.take(extended, page_table.reshape(row_count * MAXP), axis=0)  7.18 us
  transfers between devices with their start and end apart: 5, of which 2 were waited for; matrix products, arithmetic and copies ran while one was open for 21% of the time, Pallas kernels for 0%

commit v1 on v0

--- a/solution.py
+++ b/solution.py
@@ -1,6 +1,10 @@
+import functools
+
 import jax
 import jax.numpy as jnp
 from jax import lax
+from jax.experimental import pallas as pl
+from jax.experimental.pallas import tpu as pltpu
 from jax.sharding import PartitionSpec as P
 
 HEADS = 64
@@ -31,6 +35,291 @@
     cosine = jnp.cos(angle)
     sine = jnp.sin(angle)
     return jnp.concatenate([first * cosine - second * sine, second * cosine + first * sine], axis=1)
+
+
+STEP = 512
+
+
+def moe_kernel(
+    dp, n, hid, gain, amap, bmap, wt, qmap, pmap, wg, wu, wd, out,
+    wg_v, wu_v, wd_v, pack, arr, ret, xs, rs_r, rs_l, gacc, uacc, act,
+    w_sem, a_send, a_recv, b_send, b_recv, agr_send, agr_recv, agl_send, agl_recv,
+    rsr_send, rsr_recv, rsl_send, rsl_recv,
+):
+    f32 = jnp.float32
+    bf16 = jnp.bfloat16
+    me_d = lax.axis_index("dp")
+    me_e = lax.axis_index("expert")
+    mid = n // 2
+    experts, width, _ = wg_v.shape
+    half = width // 2
+    steps = half // STEP
+    block = xs.shape[2]
+    rows_e = block // experts
+
+    def ring_to_axis(p):
+        return jnp.where(p < mid, 2 * p, 2 * (n - p) - 1)
+
+    pos = jnp.where(lax.rem(me_e, 2) == 0, me_e // 2, n - (me_e + 1) // 2)
+    right = (me_d, ring_to_axis(lax.rem(pos + 1, n)))
+    left = (me_d, ring_to_axis(lax.rem(pos + n - 1, n)))
+
+    def across(k):
+        return (lax.rem(me_d + k, dp), me_e)
+
+    weights = [
+        pltpu.make_async_copy(a, b, w_sem.at[i])
+        for i, (a, b) in enumerate(((wg, wg_v), (wu, wu_v), (wd, wd_v)))
+    ]
+
+    barrier = pltpu.get_barrier_semaphore()
+    for device in [right, left] + [across(k) for k in range(1, dp)]:
+        pl.semaphore_signal(
+            barrier, inc=1, device_id=device, device_id_type=pl.DeviceIdType.MESH
+        )
+
+    def remote(src, dst, send, recv, device):
+        return pltpu.make_async_remote_copy(
+            src_ref=src,
+            dst_ref=dst,
+            send_sem=send,
+            recv_sem=recv,
+            device_id=device,
+            device_id_type=pl.DeviceIdType.MESH,
+        )
+
+    def cols(i, base=0):
+        return pl.ds(pl.multiple_of(base + i * STEP, STEP), STEP)
+
+    def square(i, total):
+        x = hid[:, cols(i)].astype(f32)
+        return total + jnp.sum(x * x, axis=1, keepdims=True)
+
+    stat = lax.fori_loop(0, 2 * steps, square, jnp.zeros((hid.shape[0], 1), f32)) / width
+    scale = lax.rsqrt(stat + norm_eps)
+
+    def pack_step(i, carry):
+        total = None
+        for h in range(2):
+            c = cols(i, h * half)
+            normed = (hid[:, c].astype(f32) * scale * gain[:, c]).astype(bf16)
+            part = jnp.dot(amap[h], normed, preferred_element_type=f32)
+            total = part if total is None else total + part
+        total = total.astype(bf16).reshape(dp, 16, STEP)
+        pack[:, :, cols(i)] = total
+        arr[0, :, cols(i)] = total[0]
+        return carry
+
+    lax.fori_loop(0, steps, pack_step, 0)
+    pl.semaphore_wait(barrier, dp + 1)
+    there = [
+        remote(pack.at[k], arr.at[k], a_send.at[k], a_recv.at[k], across(k)) for k in range(1, dp)
+    ]
+    for copy in there:
+        copy.start()
+    for copy in weights:
+        copy.start()
+    for copy in there:
+        copy.wait()
+
+    def sort_step(i, carry):
+        rows = arr[:, :, cols(i)].reshape(dp * 16, STEP)
+        for h in range(2):
+            xs[0, h, :, cols(i)] = jnp.dot(qmap[h], rows, preferred_element_type=f32).astype(bf16)
+        return carry
+
+    lax.fori_loop(0, steps, sort_step, 0)
+
+    def go_right(s, h):
+        return remote(
+            xs.at[s - 1, h], xs.at[s, h], agr_send.at[s - 1, h], agr_recv.at[s - 1, h], right
+        )
+
+    def go_left(s, h):
+        return remote(
+            xs.at[(n - s + 1) % n, h], xs.at[n - s, h], agl_send.at[s - 1, h],
+            agl_recv.at[s - 1, h], left,
+        )
+
+    sent = []
+    for s in range(1, mid + 1):
+        for h in range(2):
+            for go, last in ((go_right, 0), (go_left, 1)):
+                if s > 1:
+                    go(s - 1, h).wait_recv()
+                if s < mid or h == last:
+                    copy = go(s, h)
+                    copy.start()
+                    sent.append(copy)
+    go_right(mid, 0).wait_recv()
+    go_left(mid, 1).wait_recv()
+
+    gacc[...] = jnp.zeros_like(gacc)
+    uacc[...] = jnp.zeros_like(uacc)
+    weights[0].wait()
+    weights[1].wait()
+    for h in range(2):
+
+        def up_step(i, carry):
+            for w in range(experts):
+                rows = xs[:, h, w * rows_e : (w + 1) * rows_e, cols(i)].reshape(n * rows_e, STEP)
+                k = cols(i, h * half)
+                gacc[w] += jnp.dot(rows, wg_v[w, k, :], preferred_element_type=f32)
+                uacc[w] += jnp.dot(rows, wu_v[w, k, :], preferred_element_type=f32)
+            return carry
+
+        lax.fori_loop(0, steps, up_step, 0)
+    for w in range(experts):
+        gate = gacc[w]
+        act[w] = (gate / (1.0 + jnp.exp(-gate)) * uacc[w]).astype(bf16)
+    for copy in sent:
+        copy.wait_send()
+    weights[2].wait()
+
+    def back_right(s, h):
+        return remote(
+            xs.at[mid + s - 1, h], rs_r.at[s - 1, h], rsr_send.at[s - 1, h],
+            rsr_recv.at[s - 1, h], right,
+        )
+
+    def back_left(s, h):
+        return remote(
+            xs.at[mid - s + 1, h], rs_l.at[s - 1, h], rsl_send.at[s - 1, h],
+            rsl_recv.at[s - 1, h], left,
+        )
+
+    sent = []
+    for h in range(2):
+
+        def down_step(i, carry):
+            for w in range(experts):
+                part = jnp.dot(
+                    act[w], wd_v[w, :, cols(i, h * half)], preferred_element_type=f32
+                )
+                xs[:, h, w * rows_e : (w + 1) * rows_e, cols(i)] = part.astype(bf16).reshape(
+                    n, rows_e, STEP
+                )
+            return carry
+
+        lax.fori_loop(0, steps, down_step, 0)
+        for go in (back_right, back_left):
+            if (go is back_right) == (h == 0):
+                sent.append(go(1, h))
+            else:
+                sent.append(go(2, h))
+            sent[-1].start()
+
+    def add(slot, h, landed):
+        def add_step(i, carry):
+            c = cols(i)
+            xs[slot, h, :, c] = (xs[slot, h, :, c].astype(f32) + landed[:, c].astype(f32)).astype(
+                bf16
+            )
+            return carry
+
+        lax.fori_loop(0, steps, add_step, 0)
+
+    for s in range(2, mid + 1):
+        for h in range(2):
+            for go, first, slot, landing in (
+                (back_right, 0, mid + s - 1, rs_r),
+                (back_left, 1, mid - s + 1, rs_l),
+            ):
+                if s == 2 and h != first:
+                    continue
+                go(s - 1, h).wait_recv()
+                add(slot, h, landing.at[s - 2, h])
+                copy = go(s, h)
+                copy.start()
+                sent.append(copy)
+    for h in range(2):
+        back_right(mid, h).wait_recv()
+        back_left(mid, h).wait_recv()
+
+    def fold_step(i, carry):
+        c = cols(i)
+        total = None
+        for h in range(2):
+            mine = (
+                xs[0, h, :, c].astype(f32)
+                + rs_r[mid - 1, h, :, c].astype(f32)
+                + rs_l[mid - 1, h, :, c].astype(f32)
+            ).astype(bf16)
+            part = jnp.dot(pmap[h], mine, preferred_element_type=f32)
+            total = part if total is None else total + part
+        total = total.astype(bf16).reshape(dp, 16, STEP)
+        pack[:, :, c] = total
+        ret[0, :, c] = total[0]
+        return carry
+
+    lax.fori_loop(0, steps, fold_step, 0)
+    home = [
+        remote(pack.at[k], ret.at[k], b_send.at[k], b_recv.at[k], across(dp - k))
+        for k in range(1, dp)
+    ]
+    for copy in home:
+        copy.start()
+    for copy in home:
+        copy.wait()
+
+    def out_step(i, carry):
+        rows = ret[:, :, cols(i)].reshape(dp * 16, STEP)
+        for h in range(2):
+            c = cols(i, h * half)
+            picked = jnp.dot(bmap[h], rows, preferred_element_type=f32)
+            out[:, c] = (hid[:, c].astype(f32) + wt[...] * picked).astype(bf16)
+        return carry
+
+    lax.fori_loop(0, steps, out_step, 0)
+    for copy in sent:
+        copy.wait_send()
+
+
+def run_moe(dp, n, hidden_in, gain, amap, bmap, weight, qmap, pmap, w_gate, w_up, w_down):
+    rows, width = hidden_in.shape
+    experts, _, units = w_gate.shape
+    half = width // 2
+    mid = n // 2
+    block = experts * dp * CAP
+    bf16 = jnp.bfloat16
+    dma = pltpu.SemaphoreType.DMA
+    vmem = pl.BlockSpec(memory_space=pltpu.VMEM)
+    hbm = pl.BlockSpec(memory_space=pl.ANY)
+    return pl.pallas_call(
+        functools.partial(moe_kernel, dp, n),
+        out_shape=jax.ShapeDtypeStruct((rows, width), bf16),
+        in_specs=[vmem] * 7 + [hbm] * 3,
+        out_specs=vmem,
+        scratch_shapes=[
+            pltpu.VMEM((experts, width, units), bf16),
+            pltpu.VMEM((experts, width, units), bf16),
+            pltpu.VMEM((experts, units, width), bf16),
+            pltpu.VMEM((dp, 16, half), bf16),
+            pltpu.VMEM((dp, 16, half), bf16),
+            pltpu.VMEM((dp, 16, half), bf16),
+            pltpu.VMEM((n, 2, block, half), bf16),
+            pltpu.VMEM((mid, 2, block, half), bf16),
+            pltpu.VMEM((mid, 2, block, half), bf16),
+            pltpu.VMEM((experts, n * block // experts, units), jnp.float32),
+            pltpu.VMEM((experts, n * block // experts, units), jnp.float32),
+            pltpu.VMEM((experts, n * block // experts, units), bf16),
+            dma((3,)),
+            dma((dp,)),
+            dma((dp,)),
+            dma((dp,)),
+            dma((dp,)),
+        ]
+        + [dma((mid, 2))] * 8,
+        compiler_params=pltpu.CompilerParams(
+            collective_id=0, has_side_effects=True, vmem_limit_bytes=60 * 2**20
+        ),
+        cost_estimate=pl.CostEstimate(
+            flops=6 * n * block * width * units,
+            bytes_accessed=6 * experts * width * units,
+            transcendentals=n * block * units,
+        ),
+        name="experts",
+    )(hidden_in, gain, amap, bmap, weight, qmap, pmap, w_gate, w_up, w_down)
 
 
 def body(
@@ -53,12 +342,9 @@
     row_count = hidden_in.shape[0]
     local_experts = w_gate.shape[0]
     window = local_experts * dp_count
-    width = hidden_in.shape[1]
     flat_list = migration.reshape(dp_count * MCAP)
     outgoing = jnp.take(page_pool, flat_list, axis=0).reshape(dp_count, MCAP, page_pool.shape[1])
     incoming = lax.all_to_all(outgoing, "dp", split_axis=0, concat_axis=0, tiled=True)
-    x_wide = hidden_in.astype(jnp.float32)
-    normed = rms_rows(x_wide, norm_gain).astype(jnp.bfloat16)
     in_window = expert_ids < window
     has = jnp.any(in_window, axis=1)
     chosen = jnp.sum(jnp.where(in_window, expert_ids, 0), axis=1)
@@ -71,33 +357,33 @@
     slot = jnp.sum(rank * onehot, axis=1)
     group = chosen // local_experts
     within = chosen % local_experts
-    send_index = within * (dp_count * CAP) + group * CAP + slot
-    back_index = (group * CAP + slot) * local_experts + within
-    slot_ids = jnp.arange(window * CAP)
-    send_map = ((send_index[:, None] == slot_ids[None, :]) & has[:, None]).astype(jnp.bfloat16)
-    back_map = ((back_index[:, None] == slot_ids[None, :]) & has[:, None]).astype(jnp.bfloat16)
-    packed = jnp.einsum("rs,rd->sd", send_map, normed, preferred_element_type=jnp.float32).astype(
-        jnp.bfloat16
-    )
-    packed = packed.reshape(local_experts, dp_count * CAP, width)
-    arrived = lax.all_to_all(packed, "dp", split_axis=1, concat_axis=1, tiled=True)
-    piece = lax.all_gather(arrived, "expert", axis=1, tiled=True)
-    gate = jnp.einsum("end,edf->nef", piece, w_gate, preferred_element_type=jnp.float32)
-    upper = jnp.einsum("end,edf->nef", piece, w_up, preferred_element_type=jnp.float32)
-    active_all = (jax.nn.silu(gate) * upper).astype(jnp.bfloat16)
-    summed = lax.psum_scatter(
-        jnp.einsum("nef,efd->ned", active_all, w_down, preferred_element_type=jnp.float32).astype(
-            jnp.bfloat16
-        ),
-        "expert",
-        scatter_dimension=0,
-        tiled=True,
-    )
-    returned = lax.all_to_all(summed, "dp", split_axis=0, concat_axis=0, tiled=True)
-    picked = jnp.dot(
-        back_map, returned.reshape(window * CAP, width), preferred_element_type=jnp.float32
-    )
-    hidden_out = (x_wide + weight[:, None] * picked).astype(jnp.bfloat16)
+    apart = (group - lax.axis_index("dp") + dp_count) % dp_count
+    halves = jnp.arange(2)[:, None, None]
+    target = apart * 16 + within * CAP + slot
+    lines = jnp.arange(dp_count * 16)
+    hit = (target[None, :, None] + 8 * halves == lines[None, None, :]) & has[None, :, None]
+    back_map = hit.astype(jnp.bfloat16)
+    send_map = jnp.swapaxes(back_map, 1, 2)
+    block = local_experts * dp_count * CAP
+    places = jnp.arange(block)
+    own_expert = places // (dp_count * CAP)
+    source = places // CAP % dp_count
+    origin = source * 16 + own_expert * CAP + places % CAP
+    sort_map = (origin[None, :, None] + 8 * halves == lines[None, None, :]).astype(jnp.bfloat16)
+    hidden_out = run_moe(
+        dp_count,
+        lax.axis_size("expert"),
+        hidden_in,
+        norm_gain[None, :],
+        send_map,
+        back_map,
+        jnp.where(has, weight, 0.0)[:, None],
+        sort_map,
+        jnp.swapaxes(sort_map, 1, 2),
+        w_gate,
+        w_up,
+        w_down,
+    )
     projected = jnp.dot(
         hidden_out,
         lax.all_gather(w_latent, ("dp", "expert"), axis=0, tiled=True),

time: 259 us -> 234 us (0.903)
  Pallas kernels: 0 us -> 135 us
  waiting for transfers between devices: 125 us -> 0.71 us
  matrix products: 40.7 us -> 17.5 us
  blocking collectives: 12.2 us -> 0 us
  local copies, waits for them, and re-layouts: 42.7 us -> 46.8 us
  starting transfers between devices: 7.23 us -> 4.27 us
    pallas_call x0 -> x1, Pallas kernels: none -> 135 us  [run_moe(): pl.pallas_call(functools.partial(moe_kernel, dp, n), out_shape=jax.ShapeD...]
    all_gather x1 -> x0, waiting for transfers between devices: 67.2 us -> none  [body(): piece = lax.all_gather(arrived, 'expert', axis=1, tiled=True)]
    reduce_scatter x1 -> x0, waiting for transfers between devices: 57.1 us -> none  [body(): lax.psum_scatter(jnp.einsum('nef,efd->ned', active_all, w_down, preferred...]
    dot_general x4 -> x0, matrix products: 18.8 us -> none  [the longest x1 10.3 us: body(): jnp.einsum('nef,efd->ned', active_all, w_down, preferred_element_type=jnp...]
    all_to_all x1 -> x0, blocking collectives: 12.2 us -> none  [body(): lax.all_to_all(packed, 'dp', split_axis=1, concat_axis=1, tiled=True)]
    unnamed x20 -> x17, local copies, waits for them, and re-layouts: 6.68 us -> 11.1 us
    all_to_all x1 -> x0, starting transfers between devices: 3.65 us -> none  [body(): lax.all_to_all(summed, 'dp', split_axis=0, concat_axis=0, tiled=True)]
    dot_general x1, matrix products: 8.15 us -> 5.42 us  [body(): jnp.einsum('rhc,rtc->rht', query, keys, preferred_element_type=jnp.float32)]
  transfers between devices with their start and end apart: 5 -> 2, of which waited for: 2 -> 0; matrix products, arithmetic and copies ran while one was open for 21% -> 24% of each run, Pallas kernels for 0% -> 58%
where the time goes in v1:
time: 234 us; the launch traced here: 233 us
  Pallas kernels  135 us (58%)
  local copies, waits for them, and re-layouts  46.8 us (20%)
  matrix products  17.5 us (7%)
  between operations  14.3 us (6%)
  other arithmetic  14.1 us (6%)
  starting transfers between devices  4.27 us (2%)
    pallas_call x1, Pallas kernels, run_moe(): pl.pallas_call(functools.partial(moe_kernel, dp, n), out_shape=jax.ShapeD...  135 us
    gather x2, local copies, waits for them, and re-layouts, body(): jnp.take(extended, page_table.reshape(row_count * MAXP), axis=0)  20.7 us
    unnamed x17, local copies, waits for them, and re-layouts  11.1 us
    reshape x1, local copies, waits for them, and re-layouts, body(): query = queries.reshape(row_count, HEADS, KVW)  9.91 us
    dot_general x1, matrix products, body(): jnp.einsum('rhc,rtc->rht', query, keys, preferred_element_type=jnp.float32)  5.42 us
    dot_general x1, matrix products, body(): jnp.dot(hidden_out, lax.all_gather(w_latent, ('dp', 'expert'), axis=0, ti...  5.19 us
  transfers between devices with their start and end apart: 2, of which 0 were waited for; matrix products, arithmetic and copies ran while one was open for 24% of the time, Pallas kernels for 58%

profile of v1, /device:TPU:0, one launch (start us, length us, event | category | flops | bytes accessed | tf_op | source)
XLA Modules:
  0.0 232.9 jit_solution(4727264390570344517)
XLA Ops:
  7.9 0.8 reshape.331
  8.7 3.0 %gather_fusion = bf16[16,9216]{1,0:T(8,128)(2,1)S(1)} fusion(bf16[128,9216]{1,0:T(8,128)(2,1)} %param.24, s32[1024]{0:T(1024)S(1)} %pad_clamp_fusion.1), kind=kCustom, calls=%fused_computation | custom fusion | bytes 589888 | tf_op jit(solution)/shard_map/jit(_take)/gather | solution.py:346
  12.5 0.9 broadcast_select_fusion.1
  13.4 4.2 %all-to-all-start = ((bf16[4,4,9216]{2,1,0:T(4,128)(2,1)}), bf16[4,4,9216]{2,1,0:T(4,128)(2,1)S(1)}, u32[]{:S(2)}, u32[]{:S(2)}) async-start(bf16[4,4,9216]{2,1,0:T(4,128)(2,1)} %broadcast_select_fusion.1), calls=%async_computation | async-start | bytes 589824 | tf_op jit(solution)/shard_map/all_to_all | solution.py:347
  18.3 0.8 copy.32
  19.0 0.7 compare_and_fusion
  19.9 0.8 copy.27
  20.6 0.8 copy.29
  21.7 0.7 copy.30.wt
  24.5 0.7 fusion.16
  25.2 135.1 %experts.1 = bf16[64,7168]{1,0:T(8,128)(2,1)} custom-call(bf16[64,7168]{1,0:T(8,128)(2,1)} %hid.1, f32[1,7168]{1,0:T(1,128)} %bitcast.32, bf16[2,64,64]{2,1,0:T(8,128)(2,1)} %get-tuple-element.13.amap, bf16[2,64,64]{2,1,0:T(8,128)(2,1)} %get-tuple-element.12.bmap, f32[64,1]{1,0:T(8,128)} %copy.30.wt, bf16[2,32,64]{2,1,0:T(8,128)(2,1)} %fusion.20.qmap, ...), custom_call_target="tpu_custom_call" | custom-call | flops 2818572288 | bytes 22020096 | tf_op jit(solution)/shard_map/experts/pallas_call | solution.py:288
  160.3 9.9 %reshape.334 = bf16[64,64,576]{2,1,0:T(8,128)(2,1)} reshape(bf16[64,36864]{1,0:T(8,128)(2,1)} %param.23) | data formatting | bytes 9437184 | tf_op jit(solution)/shard_map/reshape | solution.py:401
  170.5 1.8 pad_maximum_fusion
  172.3 8.0 %gather_fusion.1 = bf16[384,9216]{1,0:T(8,128)(2,1)} fusion(bf16[144,9216]{1,0:T(8,128)(2,1)S(1)} %pad_maximum_fusion, s32[1024]{0:T(1024)S(1)} %pad_clamp_fusion), kind=kCustom, calls=%fused_computation.1 | custom fusion | bytes 14157312 | tf_op jit(solution)/shard_map/jit(_take)/gather | solution.py:398
  180.3 12.7 %gather.15 = bf16[64,96,576]{2,1,0:T(8,128)(2,1)} reshape(bf16[384,9216]{1,0:T(8,128)(2,1)} %gather_fusion.1) | data formatting | bytes 14155776 | tf_op jit(solution)/shard_map/jit(_take)/gather | solution.py:398
  193.0 4.5 %broadcast_select_fusion = bf16[64,96,576]{2,1,0:T(8,128)(2,1)S(1)} fusion(bf16[64,96,576]{2,1,0:T(8,128)(2,1)} %gather.15, pred[64,96]{1,0:T(8,128)(4,1)S(1)} %copy.31), kind=kLoop, calls=%fused_computation.3 | loop fusion | flops 3538944 | bytes 14161920 | tf_op jit(solution)/shard_map/jit(_take)/select_n | solution.py:398
  197.5 3.1 %copy-done = bf16[64,96,576]{2,1,0:T(8,128)(2,1)} copy-done((bf16[64,96,576]{2,1,0:T(8,128)(2,1)}, bf16[64,96,576]{2,1,0:T(8,128)(2,1)S(1)}, u32[]{:S(2)}) %copy-start) | copy-done | bytes 7077912
  200.6 5.4 %select_reduce_fusion = (f32[64,64]{1,0:T(8,128)S(1)}, f32[64,96,64]{1,2,0:T(8,128)S(1)}) fusion(pred[64,96]{1,0:T(8,128)(4,1)S(1)} %iota_compare_fusion.3, bf16[64,96,576]{2,1,0:T(8,128)(2,1)S(1)} %broadcast_select_fusion, bf16[64,64,576]{2,1,0:T(8,128)(2,1)} %reshape.334), kind=kOutput, calls=%fused_computation.11 | convolution fusion | flops 454160384 | bytes 13391872 | tf_op jit(solution)/shard_map/rhc,rtc->rht/dot_general | solution.py:403
  206.1 5.2 %fusion.49 = f32[64,576]{1,0:T(8,128)S(1)} fusion(bf16[64,7168]{1,0:T(8,128)(2,1)S(1)} %copy-done.2, bf16[7168,576]{1,0:T(8,128)(2,1)} %all-gather.2.cloned.1.call-done), kind=kOutput, calls=%fused_computation.108 | convolution fusion | flops 528482304 | bytes 9322496 | tf_op jit(solution)/shard_map/dot_general | solution.py:387
  212.2 4.3 %fusion.11 = f32[64,1,64]{2,1,0:T(1,128)S(1)} fusion(bf16[64,64,576]{2,1,0:T(8,128)(2,1)} %reshape.334, bf16[64,576,1]{1,0,2:T(8,128)(2,1)S(1)} %maximum_bitcast_fusion), kind=kOutput, calls=%fused_computation.18 | convolution fusion | flops 4718592 | bytes 4808704 | tf_op jit(solution)/shard_map/rhc,rc->rh/dot_general | solution.py:406
  216.6 1.3 bitcast_reduce_fusion
  217.9 2.6 %add_convert_fusion = bf16[64,64,512]{2,1,0:T(8,128)(2,1)S(1)} fusion(f32[64,512]{1,0:T(8,128)S(1)} %get-tuple-element.4, f32[64,64]{1,0:T(8,128)S(1)} %get-tuple-element.9, bf16[64,96,576]{2,1,0:T(8,128)(2,1)S(1)} %copy-done.1, f32[64,96,64]{1,2,0:T(8,128)S(1)} %get-tuple-element.15, f32[64,64]{1,0:T(8,128)S(1)} %get-tuple-element.8, ...), kind=kOutput, calls=%fused_computation.2 | convolution fusion | flops 410910720 | bytes 12820480 | tf_op jit(solution)/shard_map/rht,rtc->rhc/dot_general | solution.py:415
  220.5 4.6 %copy.41 = bf16[8,8,64,512]{3,1,2,0:T(8,128)(2,1)} copy(bf16[8,8,64,512]{3,2,1,0:T(8,128)(2,1)S(1)} %bitcast.28) | data formatting | bytes 8388608
  225.1 0.9 copy.45
  (52 shorter events, 5.7 us)
Async XLA Ops:
  7.2 198.9 %all-gather.2.cloned.1.call-start = ((), (), s32[]{:S(2)}) async-start(), calls=%async_computation.1 | async-start | bytes 9461760 | tf_op jit(solution)/shard_map/all_gather | solution.py:389
  13.4 157.0 %all-to-all-start = ((bf16[4,4,9216]{2,1,0:T(4,128)(2,1)}), bf16[4,4,9216]{2,1,0:T(4,128)(2,1)S(1)}, u32[]{:S(2)}, u32[]{:S(2)}) async-start(bf16[4,4,9216]{2,1,0:T(4,128)(2,1)} %broadcast_select_fusion.1), calls=%async_computation | async-start | bytes 589824 | tf_op jit(solution)/shard_map/all_to_all | solution.py:347
  160.3 10.0 %copy-start.4 = (s32[64]{0:T(128)S(1)}, s32[64]{0:T(128)}, u32[]{:S(2)}) copy-start(s32[64]{0:T(128)} %param.26) | copy-start | bytes 772
  197.5 3.1 %copy-start = (bf16[64,96,576]{2,1,0:T(8,128)(2,1)}, bf16[64,96,576]{2,1,0:T(8,128)(2,1)S(1)}, u32[]{:S(2)}) copy-start(bf16[64,96,576]{2,1,0:T(8,128)(2,1)S(1)} %broadcast_select_fusion) | copy-start | bytes 21233668
  200.6 5.5 %copy-start.2 = (bf16[64,7168]{1,0:T(8,128)(2,1)S(1)}, bf16[64,7168]{1,0:T(8,128)(2,1)}, u32[]{:S(2)}) copy-start(bf16[64,7168]{1,0:T(8,128)(2,1)} %experts.1) | copy-start | bytes 2752516
  206.0 6.0 %copy-start.3 = (f32[512]{0:T(512)S(1)}, f32[512]{0:T(512)}, u32[]{:S(2)}) copy-start(f32[512]{0:T(512)} %param.22) | copy-start | bytes 6148
  212.0 5.9 %copy-start.1 = (bf16[64,96,576]{2,1,0:T(8,128)(2,1)S(1)}, bf16[64,96,576]{2,1,0:T(8,128)(2,1)}, u32[]{:S(2)}) copy-start(bf16[64,96,576]{2,1,0:T(8,128)(2,1)} %copy-done) | copy-start | bytes 21233668
Sparse Core Ops, SparseCore 0:
  10.8 103.2 all-gather.1

commit v2 on v1

--- a/solution.py
+++ b/solution.py
@@ -322,6 +322,136 @@
     )(hidden_in, gain, amap, bmap, weight, qmap, pmap, w_gate, w_up, w_down)
 
 
+PAD = 640
+TABLE = 256
+SPAN = 896
+
+
+def attend_kernel(q, pick, bias, fresh, pool, moved, out, pages, keys, qs, outs):
+    f32 = jnp.float32
+    bf16 = jnp.bfloat16
+    groups = keys.shape[0]
+    listed = MAXP * 8
+    cached = listed * PAGE
+    pairs = HEADS // 2
+    extended = pool.shape[0] + moved.shape[0]
+
+    @pl.when(pl.program_id(0) == 0)
+    def _():
+        pages[...] = jnp.zeros_like(pages)
+        keys[:, cached:, :] = jnp.zeros((groups, SPAN - cached, PAD), bf16)
+        keys[:, cached : cached + 16, :] = fresh[...]
+        lane = lax.broadcasted_iota(jnp.int32, (extended, PAD), 1)
+
+        def window(start):
+            c = pl.ds(pl.multiple_of(start, 128), PAD)
+            return jnp.concatenate([pool[:, c].astype(f32), moved[:, c].astype(f32)], axis=0)
+
+        def split(i, carry):
+            even = jnp.where(lane < KVW, window(i * (2 * KVW)), 0.0)
+            odd = jnp.where(lane >= PAD - KVW, window(i * (2 * KVW) + 2 * KVW - PAD), 0.0)
+            pages[2 * i, :extended, :] = even.astype(bf16)
+            pages[2 * i + 1, :extended, :] = pltpu.roll(odd, KVW, 1).astype(bf16)
+            return carry
+
+        lax.fori_loop(0, PAGE // 2, split, 0)
+
+        def gather(u, carry):
+            rows = jnp.dot(pick[...], pages[u], preferred_element_type=f32).astype(bf16)
+            keys[:, pl.ds(pl.multiple_of(u * listed, 16), listed), :] = rows.reshape(
+                groups, listed, PAD
+            )
+            return carry
+
+        lax.fori_loop(0, PAGE, gather, 0)
+
+    for odd in range(2):
+
+        def load(i, carry):
+            start = pl.multiple_of(i * (2 * KVW) + odd * (2 * KVW - PAD), 128)
+            x = q[:, pl.ds(start, PAD)].astype(f32)
+            if odd:
+                x = pltpu.roll(x, KVW, 1)
+            at = pl.ds(pl.multiple_of(i * 8, 8), 8)
+            qs[0, at, :] = x[:8]
+            qs[1, at, :] = x[8:]
+            return carry
+
+        lax.fori_loop(0, pairs, load, 0)
+        for sub in range(2):
+            group = pl.program_id(0) * 2 + sub
+            scores = lax.dot_general(
+                qs[sub].astype(bf16),
+                keys[group],
+                (((1,), (1,)), ((), ())),
+                preferred_element_type=f32,
+            )
+            scores = (
+                scores.reshape(pairs, 8, SPAN) * softmax_scale
+                + bias[sub * 8 : sub * 8 + 8, :][None]
+            )
+            top = jnp.max(scores, axis=2, keepdims=True)
+            expo = jnp.exp(scores - top)
+            total = jnp.sum(expo, axis=2, keepdims=True)
+            probs = (expo * (1.0 / total)).reshape(pairs * 8, SPAN).astype(bf16)
+            outs[sub] = jnp.dot(probs, keys[group, :, :LATENT], preferred_element_type=f32)
+
+        def store(i, carry):
+            at = pl.ds(pl.multiple_of(i * 8, 8), 8)
+            rows = jnp.concatenate([outs[0, at, :], outs[1, at, :]], axis=0)
+            start = pl.multiple_of(i * (2 * LATENT) + odd * LATENT, 128)
+            out[:, pl.ds(start, LATENT)] = rows.astype(bf16)
+            return carry
+
+        lax.fori_loop(0, pairs, store, 0)
+
+
+def run_attend(queries, page_table, kv_lengths, new_key, page_pool, moved):
+    rows = queries.shape[0]
+    groups = rows // 8
+    listed = MAXP * 8
+    bf16 = jnp.bfloat16
+    pick = (page_table.reshape(rows * MAXP)[:, None] == jnp.arange(TABLE)[None, :]).astype(bf16)
+    place = jnp.arange(SPAN)
+    entry = place % listed
+    owner = jnp.where(place < listed * PAGE, entry // MAXP, place - listed * PAGE)
+    time = jnp.where(place < listed * PAGE, entry % MAXP * PAGE + place // listed, -1)
+    mine = (jnp.arange(rows) % 8)[:, None] == owner[None, :]
+    bias = jnp.where(mine & (time[None, :] < kv_lengths[:, None]), 0.0, -1e30)
+    fresh = jnp.pad(new_key.reshape(groups, 8, KVW), ((0, 0), (0, 8), (0, PAD - KVW)))
+
+    def whole(array):
+        return pl.BlockSpec(array.shape, lambda i: (0,) * array.ndim)
+
+    return pl.pallas_call(
+        attend_kernel,
+        grid=(rows // 16,),
+        out_shape=jax.ShapeDtypeStruct((rows, HEADS * LATENT), bf16),
+        in_specs=[
+            pl.BlockSpec((16, HEADS * KVW), lambda i: (i, 0)),
+            whole(pick),
+            pl.BlockSpec((16, SPAN), lambda i: (i, 0)),
+            whole(fresh),
+            whole(page_pool),
+            whole(moved),
+        ],
+        out_specs=pl.BlockSpec((16, HEADS * LATENT), lambda i: (i, 0)),
+        scratch_shapes=[
+            pltpu.VMEM((PAGE, TABLE, PAD), bf16),
+            pltpu.VMEM((groups, SPAN, PAD), bf16),
+            pltpu.VMEM((2, HEADS * 4, PAD), jnp.float32),
+            pltpu.VMEM((2, HEADS * 4, LATENT), jnp.float32),
+        ],
+        compiler_params=pltpu.CompilerParams(vmem_limit_bytes=56 * 2**20),
+        cost_estimate=pl.CostEstimate(
+            flops=4 * rows * HEADS * SPAN * PAD,
+            bytes_accessed=2 * rows * HEADS * (KVW + LATENT),
+            transcendentals=rows * HEADS * SPAN,
+        ),
+        name="attend",
+    )(queries, pick, bias, fresh, page_pool, moved)
+
+
 def body(
     hidden_in,
     norm_gain,
@@ -339,7 +469,6 @@
     migration,
 ):
     dp_count = lax.axis_size("dp")
-    row_count = hidden_in.shape[0]
     local_experts = w_gate.shape[0]
     window = local_experts * dp_count
     flat_list = migration.reshape(dp_count * MCAP)
@@ -384,41 +513,16 @@
         w_up,
         w_down,
     )
-    projected = jnp.dot(
-        hidden_out,
-        lax.all_gather(w_latent, ("dp", "expert"), axis=0, tiled=True),
-        preferred_element_type=jnp.float32,
-    )
+    latent_part = lax.all_gather(w_latent, "expert", axis=0, tiled=True)
+    features = lax.all_to_all(hidden_out, "dp", split_axis=1, concat_axis=0, tiled=True)
+    products = jnp.dot(features, latent_part, preferred_element_type=jnp.float32)
+    products = lax.all_to_all(products, "dp", split_axis=0, concat_axis=0, tiled=True)
+    projected = jnp.sum(products.reshape(dp_count, hidden_in.shape[0], KVW), axis=0)
     latent = rms_rows(projected[:, :LATENT], kv_gain)
     rotary = rotate_keys(projected[:, LATENT:], kv_lengths.astype(jnp.float32))
     new_key = jnp.concatenate([latent, rotary], axis=1).astype(jnp.bfloat16)
-    extended = jnp.concatenate(
-        [page_pool, incoming.reshape(dp_count * MCAP, page_pool.shape[1])], axis=0
-    )
-    keys = jnp.take(extended, page_table.reshape(row_count * MAXP), axis=0).reshape(
-        row_count, MAXP * PAGE, KVW
-    )
-    query = queries.reshape(row_count, HEADS, KVW)
-    scores = (
-        jnp.einsum("rhc,rtc->rht", query, keys, preferred_element_type=jnp.float32) * softmax_scale
-    )
-    own = (
-        jnp.einsum("rhc,rc->rh", query, new_key, preferred_element_type=jnp.float32) * softmax_scale
-    )
-    valid = jnp.arange(MAXP * PAGE)[None, None, :] < kv_lengths[:, None, None]
-    top = jnp.maximum(jnp.max(jnp.where(valid, scores, -1e30), axis=2), own)
-    expo = jnp.where(valid, jnp.exp(scores - top[:, :, None]), 0.0)
-    expo_own = jnp.exp(own - top)
-    total = jnp.sum(expo, axis=2) + expo_own
-    probs = (expo / total[:, :, None]).astype(jnp.bfloat16)
-    probs_own = (expo_own / total).astype(jnp.bfloat16)
-    result = jnp.einsum(
-        "rht,rtc->rhc", probs, keys[:, :, :LATENT], preferred_element_type=jnp.float32
-    )
-    result = result + probs_own.astype(jnp.float32)[:, :, None] * new_key[:, None, :LATENT].astype(
-        jnp.float32
-    )
-    attended = result.astype(jnp.bfloat16).reshape(row_count, HEADS * LATENT)
+    moved = incoming.reshape(dp_count * MCAP, page_pool.shape[1])
+    attended = run_attend(queries, page_table, kv_lengths, new_key, page_pool, moved)
     return (hidden_out, attended)
 
 

time: 234 us -> 237 us (1.013)
  local copies, waits for them, and re-layouts: 46.8 us -> 7.45 us
  Pallas kernels: 135 us -> 171 us
  waiting for transfers between devices: 0.71 us -> 22.1 us
  matrix products: 17.5 us -> 3.66 us
  other arithmetic: 14.1 us -> 6.64 us
  starting transfers between devices: 4.27 us -> 11.2 us
    pallas_call x0 -> x1, Pallas kernels: none -> 40.4 us  [run_attend(): pl.pallas_call(attend_kernel, grid=(rows // 16,), out_shape=jax.ShapeDtyp...]
    gather x2 -> x0, local copies, waits for them, and re-layouts: 20.7 us -> none  [body(): jnp.take(extended, page_table.reshape(row_count * MAXP), axis=0)]
    all_to_all x0 -> x2, waiting for transfers between devices: none -> 18.7 us  [the longest x1 10.9 us: body(): lax.all_to_all(hidden_out, 'dp', split_axis=1, concat_axis=0, tiled=True)]
    dot_general x4 -> x1, matrix products: 17.5 us -> 3.66 us  [body(): jnp.dot(features, latent_part, preferred_element_type=jnp.float32)]
    reshape x3 -> x1, local copies, waits for them, and re-layouts: 10.1 us -> 0.78 us  [body(): moved = incoming.reshape(dp_count * MCAP, page_pool.shape[1])]
    unnamed x17 -> x16, local copies, waits for them, and re-layouts: 11.1 us -> 2.6 us
    all_to_all x0 -> x2, starting transfers between devices: none -> 7.7 us  [the longest x1 4.21 us: body(): lax.all_to_all(hidden_out, 'dp', split_axis=1, concat_axis=0, tiled=True)]
    pallas_call x1, Pallas kernels: 135 us -> 131 us  [run_moe(): pl.pallas_call(functools.partial(moe_kernel, dp, n), out_shape=jax.ShapeD...]
  transfers between devices with their start and end apart: 2 -> 4, of which waited for: 0 -> 3; matrix products, arithmetic and copies ran while one was open for 24% -> 7% of each run, Pallas kernels for 58% -> 55%
where the time goes in v2:
time: 237 us; the launch traced here: 236 us
  Pallas kernels  171 us (72%)
  waiting for transfers between devices  22.1 us (9%)
  between operations  14.2 us (6%)
  starting transfers between devices  11.2 us (5%)
  local copies, waits for them, and re-layouts  7.45 us (3%)
  other arithmetic  6.64 us (3%)
  matrix products  3.66 us (2%)
    pallas_call x1, Pallas kernels, run_moe(): pl.pallas_call(functools.partial(moe_kernel, dp, n), out_shape=jax.ShapeD...  131 us
    pallas_call x1, Pallas kernels, run_attend(): pl.pallas_call(attend_kernel, grid=(rows // 16,), out_shape=jax.ShapeDtyp...  40.4 us
    all_to_all x1, waiting for transfers between devices, body(): lax.all_to_all(hidden_out, 'dp', split_axis=1, concat_axis=0, tiled=True)  10.9 us
    all_to_all x1, waiting for transfers between devices, body(): lax.all_to_all(products, 'dp', split_axis=0, concat_axis=0, tiled=True)  7.85 us
  transfers between devices with their start and end apart: 4, of which 3 were waited for; matrix products, arithmetic and copies ran while one was open for 7% of the time, Pallas kernels for 55%

profile of v2, /device:TPU:0, one launch (start us, length us, event | category | flops | bytes accessed | tf_op | source)
XLA Modules:
  0.0 236.2 jit_solution(11729288582076128025)
XLA Ops:
  7.2 0.7 all-gather.2.cloned.1.call-update
  8.0 0.7 fusion.29.qmap
  8.7 0.6 fusion.18.pmap
  9.3 0.8 copy.21
  10.7 0.8 copy.23
  11.6 0.7 copy.24.wt
  12.4 0.7 fusion.17
  13.1 130.5 %experts.1 = bf16[64,7168]{1,0:T(8,128)(2,1)} custom-call(bf16[64,7168]{1,0:T(8,128)(2,1)} %hid.1, f32[1,7168]{1,0:T(1,128)} %bitcast.26, bf16[2,64,64]{2,1,0:T(8,128)(2,1)} %get-tuple-element.7.amap, bf16[2,64,64]{2,1,0:T(8,128)(2,1)} %get-tuple-element.6.bmap, f32[64,1]{1,0:T(8,128)} %copy.24.wt, bf16[2,32,64]{2,1,0:T(8,128)(2,1)} %fusion.29.qmap, ...), custom_call_target="tpu_custom_call" | custom-call | flops 2818572288 | bytes 22020096 | tf_op jit(solution)/shard_map/experts/pallas_call | solution.py:288
  143.7 2.3 copy.29
  146.0 4.2 %all-to-all-start = ((bf16[64,4,1792]{2,0,1:T(8,128)(2,1)}), bf16[64,4,1792]{2,0,1:T(8,128)(2,1)}, u32[]{:S(2)}, u32[]{:S(2)}) async-start(bf16[64,4,1792]{2,0,1:T(8,128)(2,1)} %bitcast.24), calls=%async_computation | async-start | bytes 1835008 | tf_op jit(solution)/shard_map/all_to_all | solution.py:517
  150.3 0.7 gather_fusion
  151.2 0.9 broadcast_select_fusion
  152.4 10.9 %all-to-all-done = bf16[64,4,1792]{2,0,1:T(8,128)(2,1)} async-done(((bf16[64,4,1792]{2,0,1:T(8,128)(2,1)}), bf16[64,4,1792]{2,0,1:T(8,128)(2,1)}, u32[]{:S(2)}, u32[]{:S(2)}) %all-to-all-start) | async-done | bytes 917536 | tf_op jit(solution)/shard_map/all_to_all | solution.py:517
  163.3 3.5 %all-to-all-start.2 = ((bf16[4,4,9216]{2,1,0:T(4,128)(2,1)}), bf16[4,4,9216]{2,1,0:T(4,128)(2,1)S(1)}, u32[]{:S(2)}, u32[]{:S(2)}) async-start(bf16[4,4,9216]{2,1,0:T(4,128)(2,1)} %broadcast_select_fusion), calls=%async_computation.2 | async-start | bytes 589824 | tf_op jit(solution)/shard_map/all_to_all | solution.py:476
  166.8 3.7 %fusion = f32[4,64,576]{2,1,0:T(8,128)} fusion(bf16[1792,576]{1,0:T(8,128)(2,1)} %all-gather.2.cloned.1.call-done, bf16[64,4,1792]{2,0,1:T(8,128)(2,1)} %all-to-all-done), kind=kOutput, calls=%fused_computation.1 | convolution fusion | flops 528482304 | bytes 3571712 | tf_op jit(solution)/shard_map/dot_general | solution.py:518
  170.5 2.7 %all-to-all-done.2 = bf16[4,4,9216]{2,1,0:T(4,128)(2,1)S(1)} async-done(((bf16[4,4,9216]{2,1,0:T(4,128)(2,1)}), bf16[4,4,9216]{2,1,0:T(4,128)(2,1)S(1)}, u32[]{:S(2)}, u32[]{:S(2)}) %all-to-all-start.2) | async-done | bytes 294944 | tf_op jit(solution)/shard_map/all_to_all | solution.py:476
  173.1 3.5 %all-to-all-start.1 = ((f32[4,64,576]{2,1,0:T(8,128)}), f32[4,64,576]{2,1,0:T(8,128)S(1)}, u32[]{:S(2)}, u32[]{:S(2)}) async-start(f32[4,64,576]{2,1,0:T(8,128)} %fusion), calls=%async_computation.1 | async-start | bytes 1310720 | tf_op jit(solution)/shard_map/all_to_all | solution.py:519
  176.6 0.8 fusion.3.pick
  177.4 0.8 and_select_fusion.bias
  178.2 0.8 reshape.326.moved
  179.0 7.9 %all-to-all-done.1 = f32[4,64,576]{2,1,0:T(8,128)S(1)} async-done(((f32[4,64,576]{2,1,0:T(8,128)}), f32[4,64,576]{2,1,0:T(8,128)S(1)}, u32[]{:S(2)}, u32[]{:S(2)}) %all-to-all-start.1) | async-done | bytes 589856 | tf_op jit(solution)/shard_map/all_to_all | solution.py:519
  187.3 0.7 fusion.12.fresh
  188.1 40.4 %attend.1 = bf16[64,32768]{1,0:T(8,128)(2,1)} custom-call(bf16[64,36864]{1,0:T(8,128)(2,1)} %q.1, bf16[384,256]{1,0:T(8,128)(2,1)} %fusion.3.pick, f32[64,896]{1,0:T(8,128)} %and_select_fusion.bias, bf16[8,16,640]{2,1,0:T(8,128)(2,1)} %fusion.12.fresh, bf16[128,9216]{1,0:T(8,128)(2,1)} %pool.1, bf16[16,9216]{1,0:T(8,128)(2,1)} %reshape.326.moved), custom_call_target="tpu_custom_call" | custom-call | flops 9395240960 | bytes 8912896 | tf_op jit(solution)/shard_map/attend/pallas_call | solution.py:426
  228.5 0.9 copy.31
  (42 shorter events, 1.9 us)
Async XLA Ops:
  7.2 159.6 %all-gather.2.cloned.1.call-start = ((), (), s32[]{:S(2)}) async-start(), calls=%async_computation.3 | async-start | bytes 2580480 | tf_op jit(solution)/shard_map/all_gather | solution.py:516
  143.6 6.6 %copy-start.2 = (s32[1,1,4,4]{3,2,1,0:T(4,128)S(1)}, s32[1,1,4,4]{3,2,1,0:T(4,128)}, u32[]{:S(2)}) copy-start(s32[1,1,4,4]{3,2,1,0:T(4,128)} %param.27) | copy-start | bytes 196
  143.7 6.7 %copy-start.1 = (bf16[128,9216]{1,0:T(8,128)(2,1)S(1)}, bf16[128,9216]{1,0:T(8,128)(2,1)}, u32[]{:S(2)}) copy-start(bf16[128,9216]{1,0:T(8,128)(2,1)} %pool.1) | copy-start | bytes 7077892
  146.0 17.3 %all-to-all-start = ((bf16[64,4,1792]{2,0,1:T(8,128)(2,1)}), bf16[64,4,1792]{2,0,1:T(8,128)(2,1)}, u32[]{:S(2)}, u32[]{:S(2)}) async-start(bf16[64,4,1792]{2,0,1:T(8,128)(2,1)} %bitcast.24), calls=%async_computation | async-start | bytes 1835008 | tf_op jit(solution)/shard_map/all_to_all | solution.py:517
  150.2 1.9 copy-start.5
  150.2 1.9 copy-start.3
  163.3 9.8 %all-to-all-start.2 = ((bf16[4,4,9216]{2,1,0:T(4,128)(2,1)}), bf16[4,4,9216]{2,1,0:T(4,128)(2,1)S(1)}, u32[]{:S(2)}, u32[]{:S(2)}) async-start(bf16[4,4,9216]{2,1,0:T(4,128)(2,1)} %broadcast_select_fusion), calls=%async_computation.2 | async-start | bytes 589824 | tf_op jit(solution)/shard_map/all_to_all | solution.py:476
  170.5 16.7 %copy-start.4 = (f32[512]{0:T(512)S(1)}, f32[512]{0:T(512)}, u32[]{:S(2)}) copy-start(f32[512]{0:T(512)} %param.22) | copy-start | bytes 6148
  173.1 13.7 %all-to-all-start.1 = ((f32[4,64,576]{2,1,0:T(8,128)}), f32[4,64,576]{2,1,0:T(8,128)S(1)}, u32[]{:S(2)}, u32[]{:S(2)}) async-start(f32[4,64,576]{2,1,0:T(8,128)} %fusion), calls=%async_computation.1 | async-start | bytes 1310720 | tf_op jit(solution)/shard_map/all_to_all | solution.py:519
  188.1 40.4 %copy-start = (bf16[64,7168]{1,0:T(8,128)(2,1)S(1)}, bf16[64,7168]{1,0:T(8,128)(2,1)}, u32[]{:S(2)}) copy-start(bf16[64,7168]{1,0:T(8,128)(2,1)} %experts.1) | copy-start | bytes 2752516
Sparse Core Ops, SparseCore 0:
  10.2 71.7 all-gather.1

commit v3 on v2

--- a/solution.py
+++ b/solution.py
@@ -377,7 +377,7 @@
             qs[1, at, :] = x[8:]
             return carry
 
-        lax.fori_loop(0, pairs, load, 0)
+        lax.fori_loop(0, pairs, load, 0, unroll=4)
         for sub in range(2):
             group = pl.program_id(0) * 2 + sub
             scores = lax.dot_general(
@@ -403,7 +403,7 @@
             out[:, pl.ds(start, LATENT)] = rows.astype(bf16)
             return carry
 
-        lax.fori_loop(0, pairs, store, 0)
+        lax.fori_loop(0, pairs, store, 0, unroll=4)
 
 
 def run_attend(queries, page_table, kv_lengths, new_key, page_pool, moved):
@@ -513,11 +513,11 @@
         w_up,
         w_down,
     )
-    latent_part = lax.all_gather(w_latent, "expert", axis=0, tiled=True)
-    features = lax.all_to_all(hidden_out, "dp", split_axis=1, concat_axis=0, tiled=True)
-    products = jnp.dot(features, latent_part, preferred_element_type=jnp.float32)
-    products = lax.all_to_all(products, "dp", split_axis=0, concat_axis=0, tiled=True)
-    projected = jnp.sum(products.reshape(dp_count, hidden_in.shape[0], KVW), axis=0)
+    projected = jnp.dot(
+        hidden_out,
+        lax.all_gather(w_latent, ("dp", "expert"), axis=0, tiled=True),
+        preferred_element_type=jnp.float32,
+    )
     latent = rms_rows(projected[:, :LATENT], kv_gain)
     rotary = rotate_keys(projected[:, LATENT:], kv_lengths.astype(jnp.float32))
     new_key = jnp.concatenate([latent, rotary], axis=1).astype(jnp.bfloat16)

time: 237 us -> 207 us (0.87)
  waiting for transfers between devices: 22.1 us -> 0.69 us
  starting transfers between devices: 11.2 us -> 4.27 us
  Pallas kernels: 171 us -> 166 us
    all_to_all x2 -> x0, waiting for transfers between devices: 18.7 us -> none  [the longest x1 10.9 us: body(): lax.all_to_all(hidden_out, 'dp', split_axis=1, concat_axis=0, tiled=True)]
    pallas_call x1, Pallas kernels: 40.4 us -> 32.1 us  [run_attend(): pl.pallas_call(attend_kernel, grid=(rows // 16,), out_shape=jax.ShapeDtyp...]
    all_to_all x2 -> x0, starting transfers between devices: 7.7 us -> none  [the longest x1 4.21 us: body(): lax.all_to_all(hidden_out, 'dp', split_axis=1, concat_axis=0, tiled=True)]
    pallas_call x1, Pallas kernels: 131 us -> 134 us  [run_moe(): pl.pallas_call(functools.partial(moe_kernel, dp, n), out_shape=jax.ShapeD...]
    all_to_all x1, waiting for transfers between devices: 2.66 us -> 0.01 us  [body(): lax.all_to_all(outgoing, 'dp', split_axis=0, concat_axis=0, tiled=True)]
  transfers between devices with their start and end apart: 4 -> 2, of which waited for: 3 -> 0; matrix products, arithmetic and copies ran while one was open for 7% -> 7% of each run, Pallas kernels for 55% -> 65%
where the time goes in v3:
time: 207 us
  Pallas kernels  166 us (80%)
  between operations  14.1 us (7%)
  local copies, waits for them, and re-layouts  8.72 us (4%)
  other arithmetic  7.91 us (4%)
  matrix products  5.49 us (3%)
  starting transfers between devices  4.27 us (2%)
    pallas_call x1, Pallas kernels, run_moe(): pl.pallas_call(functools.partial(moe_kernel, dp, n), out_shape=jax.ShapeD...  134 us
    pallas_call x1, Pallas kernels, run_attend(): pl.pallas_call(attend_kernel, grid=(rows // 16,), out_shape=jax.ShapeDtyp...  32.1 us
    dot_general x1, matrix products, body(): jnp.dot(hidden_out, lax.all_gather(w_latent, ('dp', 'expert'), axis=0, ti...  5.49 us
    all_to_all x1, starting transfers between devices, body(): lax.all_to_all(outgoing, 'dp', split_axis=0, concat_axis=0, tiled=True)  4.24 us
  transfers between devices with their start and end apart: 2, of which 0 were waited for; matrix products, arithmetic and copies ran while one was open for 7% of the time, Pallas kernels for 65%

profile of v3, /device:TPU:0, one launch (start us, length us, event | category | flops | bytes accessed | tf_op | source)
XLA Modules:
  0.0 207.1 jit_solution(13041112747289270321)
XLA Ops:
  7.2 0.7 all-gather.2.cloned.1.call-update
  7.9 0.8 reshape.316
  8.7 3.0 %gather_fusion = bf16[16,9216]{1,0:T(8,128)(2,1)S(1)} fusion(bf16[128,9216]{1,0:T(8,128)(2,1)} %pool.1, s32[1024]{0:T(1024)S(1)} %pad_clamp_fusion), kind=kCustom, calls=%fused_computation | custom fusion | bytes 589888 | tf_op jit(solution)/shard_map/jit(_take)/gather | solution.py:475
  11.8 0.7 compare_and_fusion
  12.5 0.9 broadcast_select_fusion
  13.4 4.2 %all-to-all-start = ((bf16[4,4,9216]{2,1,0:T(4,128)(2,1)}), bf16[4,4,9216]{2,1,0:T(4,128)(2,1)S(1)}, u32[]{:S(2)}, u32[]{:S(2)}) async-start(bf16[4,4,9216]{2,1,0:T(4,128)(2,1)} %broadcast_select_fusion), calls=%async_computation | async-start | bytes 589824 | tf_op jit(solution)/shard_map/all_to_all | solution.py:476
  17.6 0.8 copy.20
  18.4 0.8 copy.22
  19.4 0.7 copy.23.wt
  20.1 0.7 convert_element_type.29
  20.8 0.8 copy.24
  22.0 0.2 select_reduce_fusion.1
  22.4 0.7 fusion.26.qmap
  23.0 0.6 fusion.15.pmap
  23.7 0.7 fusion.14
  24.4 133.7 %experts.1 = bf16[64,7168]{1,0:T(8,128)(2,1)} custom-call(bf16[64,7168]{1,0:T(8,128)(2,1)} %hid.1, f32[1,7168]{1,0:T(1,128)} %bitcast.17, bf16[2,64,64]{2,1,0:T(8,128)(2,1)} %get-tuple-element.7.amap, bf16[2,64,64]{2,1,0:T(8,128)(2,1)} %get-tuple-element.6.bmap, f32[64,1]{1,0:T(8,128)} %copy.23.wt, bf16[2,32,64]{2,1,0:T(8,128)(2,1)} %fusion.26.qmap, ...), custom_call_target="tpu_custom_call" | custom-call | flops 2818572288 | bytes 22020096 | tf_op jit(solution)/shard_map/experts/pallas_call | solution.py:288
  158.2 0.8 and_select_fusion.bias
  158.9 0.8 fusion.pick
  159.7 0.8 reshape.317.moved
  160.5 5.5 %fusion.61 = f32[64,576]{1,0:T(8,128)S(1)} fusion(bf16[64,7168]{1,0:T(8,128)(2,1)} %experts.1, bf16[7168,576]{1,0:T(8,128)(2,1)} %all-gather.2.cloned.1.call-done), kind=kOutput, calls=%fused_computation.119 | convolution fusion | flops 528482304 | bytes 9322496 | tf_op jit(solution)/shard_map/dot_general | solution.py:516
  166.2 0.2 fusion.28
  166.4 0.7 fusion.9.fresh
  167.2 32.1 %attend.1 = bf16[64,32768]{1,0:T(8,128)(2,1)} custom-call(bf16[64,36864]{1,0:T(8,128)(2,1)} %q.1, bf16[384,256]{1,0:T(8,128)(2,1)} %fusion.pick, f32[64,896]{1,0:T(8,128)} %and_select_fusion.bias, bf16[8,16,640]{2,1,0:T(8,128)(2,1)} %fusion.9.fresh, bf16[128,9216]{1,0:T(8,128)(2,1)} %pool.1, bf16[16,9216]{1,0:T(8,128)(2,1)} %reshape.317.moved), custom_call_target="tpu_custom_call" | custom-call | flops 9395240960 | bytes 8912896 | tf_op jit(solution)/shard_map/attend/pallas_call | solution.py:426
  199.3 0.9 copy.26
  (30 shorter events, 1.3 us)
Async XLA Ops:
  7.2 153.4 %all-gather.2.cloned.1.call-start = ((), (), s32[]{:S(2)}) async-start(), calls=%async_computation.1 | async-start | bytes 9461760 | tf_op jit(solution)/shard_map/all_gather | solution.py:518
  13.4 146.4 %all-to-all-start = ((bf16[4,4,9216]{2,1,0:T(4,128)(2,1)}), bf16[4,4,9216]{2,1,0:T(4,128)(2,1)S(1)}, u32[]{:S(2)}, u32[]{:S(2)}) async-start(bf16[4,4,9216]{2,1,0:T(4,128)(2,1)} %broadcast_select_fusion), calls=%async_computation | async-start | bytes 589824 | tf_op jit(solution)/shard_map/all_to_all | solution.py:476
  24.4 133.8 %copy-start.2 = (s32[64]{0:T(128)S(1)}, s32[64]{0:T(128)}, u32[]{:S(2)}) copy-start(s32[64]{0:T(128)} %param.26) | copy-start | bytes 772
  160.5 5.6 %copy-start.1 = (f32[512]{0:T(512)S(1)}, f32[512]{0:T(512)}, u32[]{:S(2)}) copy-start(f32[512]{0:T(512)} %param.22) | copy-start | bytes 6148
  167.2 32.1 %copy-start = (bf16[64,7168]{1,0:T(8,128)(2,1)S(1)}, bf16[64,7168]{1,0:T(8,128)(2,1)}, u32[]{:S(2)}) copy-start(bf16[64,7168]{1,0:T(8,128)(2,1)} %experts.1) | copy-start | bytes 2752516
Sparse Core Ops, SparseCore 0:
  10.8 102.1 all-gather.1
